TPU v7x, 32 devices: a whole 2x2x4 slice. The times are simulated.
32 devices in a mesh: grp: 2 (over y), row: 4 (over z), det: 2 (over x), sub: 2 (over core).
Axes of the slice: x: 2, y: 2, z: 4, core: 2. Of those that a mesh axis runs over, the one named last changes fastest.
Arguments:
- patterns: float32 [8, 4096, 512], P(('grp', 'row'), ('det', 'sub')), parts along dimension 0, may hold values from -6 to 6
- jitter: int32 [8], P(('grp', 'row')), parts along dimension 0, may hold values from -8 to 8
- subpixel: int32 [8], P(('grp', 'row')), parts along dimension 0, may hold values from 0 to 15
- kernels: float32 [16, 4], replicated, may hold values from -3 to 3
- intersection: int32 [4, 4, 4], P(('det', 'sub'), None, 'row'), may hold values 0 or 1
- owners: int32 [4, 4, 1], P(('det', 'sub')), may hold values from 0 to 3; in each aligned block of 4 rows (0 to 3, 4 to 7, ..., all dimensions but the last counted through in order) at most 2 rows name the same one
- wigner: float32 [2, 64, 64], replicated, may hold values from -6 to 6
Outputs:
- object_slots: float32 [8, 4, 2, 64, 256], P(('grp', 'det', 'sub'), 'row'), parts along dimension 0
There are 2 independent parts, one for each index of `grp`. A program takes and returns all parts, laid end to end along the dimension named above; an argument that names none is the same for every part. Nothing has to cross between parts.
Inputs may be any that keep to these rules, and one draw needn't show every extreme that they name: For each s, no owner appears more than 2 times among owners[s, :, 0]; some owner appears exactly 2 times in some s.
All inputs are finite; a program needn't handle non-finite values. No bound on the sum of `intersection` on one device may be relied on, other than what follows from the above.
Results may differ from a plain program's by a relative error of at most 0.0003.
Values sent between devices are 32-bit elements; how exact they have to be, the bound alone decides.
A program may use at most 128 MiB of HBM per device.

v0:
```python
import functools
import math

import jax
import jax.numpy as jnp
import numpy as np
from jax import lax
from jax.experimental import pallas as pl
from jax.experimental.pallas import tpu as pltpu
from jax.sharding import PartitionSpec as P

CAP = 2
SHIFTS = 32

highest = lax.Precision.HIGHEST
f32 = jnp.float32
bf16 = jnp.bfloat16


def slot_table(column, owners_count, capacity):
    positions = jnp.arange(column.shape[0], dtype=jnp.int32)
    earlier = (column[:, None] == column[None, :]) & (positions[:, None] < positions[None, :])
    ranking = jnp.sum(earlier.astype(jnp.int32), axis=0)
    matches = (
        column[None, None, :] == jnp.arange(owners_count, dtype=jnp.int32)[:, None, None]
    ) & (ranking[None, None, :] == jnp.arange(capacity, dtype=jnp.int32)[None, :, None])
    return matches.astype(f32)


def unit_circle(products, length):
    angles = 2.0 * np.pi / length * np.mod(products, length)
    return np.cos(angles), np.sin(angles)


def fast_tables(length, groups, scan_rows):
    samples = np.arange(length)
    cosine, sine = unit_circle(samples[:, None] * samples[None, :], length)
    scale = 1.0 / math.sqrt(length * scan_rows)
    both = np.stack([cosine, sine]).reshape(2, length, groups, length // groups)
    return (both.transpose(2, 1, 0, 3) * scale).reshape(groups, length, -1).astype(np.float32)


def inner_table(width, repeats):
    index = np.arange(width)
    cosine, sine = unit_circle(index[:, None] * index[None, :], width)
    return np.concatenate([np.tile(cosine, repeats), np.tile(sine, repeats)], 1).astype(np.float32)


def row_tables(height, width, groups):
    pixels = np.arange(height * width)
    cosine, sine = unit_circle(np.arange(height)[:, None] * (pixels // width)[None, :], height)
    both = np.stack([cosine, sine]) / math.sqrt(height * width * width)
    return both.reshape(2, height, groups, -1).transpose(2, 0, 1, 3).astype(np.float32)


def shift_tables(length, groups):
    shifts = np.arange(SHIFTS) - SHIFTS // 2
    cosine, sine = unit_circle(shifts[:, None] * np.arange(length)[None, :], length)
    both = np.stack([cosine, sine]).reshape(2, SHIFTS, groups, length // groups)
    return both.transpose(2, 0, 1, 3).astype(np.float32)


def wiener_parts(real, imaginary):
    denominator = real * real + imaginary * imaginary + 0.1
    return real / denominator, -imaginary / denominator


def general(patterns, jitter, subpixel, kernels, intersection, owners, wigner):
    _, pixel_share, length = patterns.shape
    height, width = wigner.shape[1:]
    groups = lax.axis_size(("det", "sub"))
    rows = lax.axis_size("row")
    columns = length // groups
    block_pixels = pixel_share * groups // rows
    local_blocks = pixel_share // block_pixels
    scan_rows = owners.shape[1]
    group = lax.axis_index(("det", "sub"))
    dot = functools.partial(jnp.einsum, precision=highest)

    filter_real, filter_imaginary = wiener_parts(wigner[0], wigner[1])
    repeats = pixel_share // width
    table = jnp.asarray(inner_table(width, 1))
    cosine, sine = table[:, :width], table[:, width:]
    inner_real = dot("rx,xk->rk", filter_real, cosine) + dot("rx,xk->rk", filter_imaginary, sine)
    inner_imaginary = dot("rx,xk->rk", filter_imaginary, cosine) - dot("rx,xk->rk", filter_real, sine)
    inner_real, inner_imaginary = (jnp.tile(v, (1, repeats)) for v in (inner_real, inner_imaginary))
    turn = lax.dynamic_index_in_dim(jnp.asarray(row_tables(height, width, groups)), group, 0, False)
    matrix = jnp.concatenate(
        [inner_real * turn[0] + inner_imaginary * turn[1], inner_imaginary * turn[0] - inner_real * turn[1]]
    )
    folded = dot(
        "rnp,npx->nrx",
        matrix.reshape(2 * height, local_blocks, block_pixels),
        patterns[0].reshape(local_blocks, block_pixels, length),
    )
    selector = (jnp.arange(kernels.shape[0], dtype=jnp.int32) == subpixel[0]).astype(f32)
    weights = dot("k,kt->t", selector, kernels)
    taps = kernels.shape[1]
    moved = sum(
        weights[t] * jnp.roll(folded, -(jitter[0] + t - taps // 2), axis=2) for t in range(taps)
    )
    spectrum = dot("nrx,gxf->gnrf", moved, jnp.asarray(fast_tables(length, groups, scan_rows)))
    upper, lower = spectrum[:, :, :height], spectrum[:, :, height:]
    spectrum = jnp.concatenate(
        [upper[..., :columns] + lower[..., columns:], lower[..., :columns] - upper[..., columns:]], 3
    )
    gathered = lax.all_to_all(spectrum, ("det", "sub"), split_axis=0, concat_axis=1, tiled=True)[0]
    visible = lax.all_gather(intersection[0], "row", axis=1, tiled=True).astype(f32)
    masked = dot("qb,brf->qrf", visible, gathered)
    cosine, sine = unit_circle(np.arange(scan_rows)[:, None] * np.arange(rows)[None, :], rows)
    me = lax.axis_index("row")
    cosine = jnp.asarray(cosine, f32)[:, me][:, None, None]
    sine = jnp.asarray(sine, f32)[:, me][:, None, None]
    real, imaginary = masked[..., :columns], masked[..., columns:]
    turned = jnp.concatenate([cosine * real + sine * imaginary, cosine * imaginary - sine * real], 2)
    slots = dot("ocq,qrf->ocrf", slot_table(owners[0, :, 0], rows, CAP), turned)
    return lax.psum_scatter(slots, "row", scatter_dimension=0, tiled=True)[None]


def split(value):
    high = value.astype(bf16)
    return high, (value - high.astype(f32)).astype(bf16)


def times(a, b):
    return jnp.dot(a, b, preferred_element_type=f32)


def scaled(factor, value):
    if abs(factor) < 1e-9:
        return None
    if abs(factor - 1.0) < 1e-9:
        return value
    return value * np.float32(factor)


def added(terms):
    terms = [term for term in terms if term is not None]
    return functools.reduce(lambda a, b: a + b, terms)


def fused_kernel(
    sizes, patterns, jitter, subpixel, kernels, intersection, owners, wigner, inner, turns,
    fast_high, fast_low, phases, out, pixels, turn, table_high, table_low, outgoing, incoming,
    visible, slots, load_sem, send_sem, recv_sem, mask_send, mask_recv, slot_send, slot_recv,
):
    rows, groups, subs, scan_rows, height, columns, chunks = sizes
    row = lax.axis_index("row")
    group = lax.axis_index("det") * subs + lax.axis_index("sub")
    part = height // rows
    peers = [(dr, dg) for dg in range(groups) for dr in range(rows) if (dr, dg) != (0, 0)]

    def row_at(offset):
        return lax.rem(row + offset, rows)

    def group_at(offset):
        return lax.rem(group + offset, groups)

    def device(dr, dg):
        other = group_at(dg)
        return {"row": row_at(dr), "det": other // subs, "sub": lax.rem(other, subs)}

    def rows_of(index):
        return pl.ds(pl.multiple_of(index * part, part), part)

    chunk = pixels.shape[0] // chunks
    loads = [
        pltpu.make_async_copy(turns.at[group], turn, load_sem.at[0]),
        pltpu.make_async_copy(fast_high, table_high, load_sem.at[1]),
        pltpu.make_async_copy(fast_low, table_low, load_sem.at[2]),
    ]
    pieces = [
        pltpu.make_async_copy(
            patterns.at[0, pl.ds(k * chunk, chunk)], pixels.at[pl.ds(k * chunk, chunk)], load_sem.at[3 + k]
        )
        for k in range(chunks)
    ]
    loads[0].start()
    for piece in pieces:
        piece.start()
    loads[1].start()
    loads[2].start()

    barrier = pltpu.get_barrier_semaphore()
    for dr, dg in peers:
        pl.semaphore_signal(
            barrier, inc=1, device_id=device(dr, dg), device_id_type=pl.DeviceIdType.MESH
        )

    filter_real, filter_imaginary = wiener_parts(wigner[0], wigner[1])
    both = jnp.dot(
        jnp.concatenate([filter_real, filter_imaginary]), inner[...],
        precision=highest, preferred_element_type=f32,
    )
    lanes = inner.shape[1] // 2
    inner_real = both[:height, :lanes] + both[height:, lanes:]
    inner_imaginary = both[height:, :lanes] - both[:height, lanes:]
    loads[0].wait()
    matrix = []
    for k in range(pixels.shape[0] // lanes):
        cosine = turn[0, :, k * lanes : (k + 1) * lanes]
        sine = turn[1, :, k * lanes : (k + 1) * lanes]
        matrix.append(
            split(
                jnp.concatenate(
                    [inner_real * cosine + inner_imaginary * sine, inner_imaginary * cosine - inner_real * sine]
                )
            )
        )
    per_chunk = chunk // lanes
    folded = jnp.zeros((2 * height, pixels.shape[1]), f32)
    for k in range(chunks):
        mine = matrix[k * per_chunk : (k + 1) * per_chunk]
        high = jnp.concatenate([m[0] for m in mine], 1)
        low = jnp.concatenate([m[1] for m in mine], 1)
        pieces[k].wait()
        piece_high, piece_low = split(pixels[k * chunk : (k + 1) * chunk, :])
        folded = folded + (times(high, piece_high) + times(high, piece_low) + times(low, piece_high))
    folded_high, folded_low = split(folded)

    shifts = lax.broadcasted_iota(jnp.int32, (SHIFTS, columns), 0) - SHIFTS // 2
    taps = kernels.shape[1]
    weight = jnp.zeros((SHIFTS, columns), f32)
    for t in range(taps):
        weight = weight + jnp.where(
            shifts == jitter[0] + (t - taps // 2), kernels[subpixel[0], t], 0.0
        )

    frequency = lax.broadcasted_iota(jnp.int32, visible.shape[1:], 0)
    tile = jnp.zeros(visible.shape[1:], f32)
    for q in range(scan_rows):
        tile = jnp.where(frequency == q, intersection[0, q, 0].astype(f32), tile)
    visible[row] = tile

    pl.semaphore_wait(barrier, len(peers))
    masks = []
    for dr in range(1, rows):
        copy = pltpu.make_async_remote_copy(
            src_ref=visible.at[row], dst_ref=visible.at[row], send_sem=mask_send.at[dr],
            recv_sem=mask_recv.at[row], device_id=device(dr, 0), device_id_type=pl.DeviceIdType.MESH,
        )
        copy.start()
        masks.append(copy)

    loads[1].wait()
    loads[2].wait()
    sends = []
    for dg in list(range(1, groups)) + [0]:
        other = group_at(dg)
        high = table_high[other]
        product = times(folded_high, high) + times(folded_high, table_low[other]) + times(folded_low, high)
        real = product[:height, :columns] + product[height:, columns:]
        imaginary = product[height:, :columns] - product[:height, columns:]
        phase_real = jnp.sum(weight * phases[other, 0], axis=0, keepdims=True)
        phase_imaginary = jnp.sum(weight * phases[other, 1], axis=0, keepdims=True)
        outgoing[dg, :, :columns] = real * phase_real - imaginary * phase_imaginary
        outgoing[dg, :, columns:] = real * phase_imaginary + imaginary * phase_real
        for dr in range(rows):
            if (dr, dg) == (0, 0):
                incoming[row, group] = outgoing[0, rows_of(row), :]
                continue
            copy = pltpu.make_async_remote_copy(
                src_ref=outgoing.at[dg, rows_of(row_at(dr)), :], dst_ref=incoming.at[row, group],
                send_sem=send_sem.at[dr, dg], recv_sem=recv_sem.at[row, group],
                device_id=device(dr, dg), device_id_type=pl.DeviceIdType.MESH,
            )
            copy.start()
            sends.append(copy)

    for dr in range(1, rows):
        pltpu.make_async_remote_copy(
            src_ref=visible.at[row_at(dr)], dst_ref=visible.at[row_at(dr)], send_sem=mask_send.at[dr],
            recv_sem=mask_recv.at[row_at(dr)], device_id=device(dr, 0), device_id_type=pl.DeviceIdType.MESH,
        ).wait_recv()
    for dr, dg in peers:
        pltpu.make_async_remote_copy(
            src_ref=outgoing.at[dg, rows_of(row), :], dst_ref=incoming.at[row_at(dr), group_at(dg)],
            send_sem=send_sem.at[dr, dg], recv_sem=recv_sem.at[row_at(dr), group_at(dg)],
            device_id=device(dr, dg), device_id_type=pl.DeviceIdType.MESH,
        ).wait_recv()

    real = [None] * scan_rows
    imaginary = [None] * scan_rows
    for b in range(groups):
        values = [incoming[y, b] for y in range(rows)]
        reals = [v[:, :columns] for v in values]
        imaginaries = [v[:, columns:] for v in values]
        for q in range(scan_rows):
            circle = [unit_circle(np.array(q * y), rows) for y in range(rows)]
            keep = visible[b, q : q + 1, :]
            sum_real = added(
                [scaled(c, v) for (c, _), v in zip(circle, reals)]
                + [scaled(s, v) for (_, s), v in zip(circle, imaginaries)]
            )
            sum_imaginary = added(
                [scaled(c, v) for (c, _), v in zip(circle, imaginaries)]
                + [scaled(-s, v) for (_, s), v in zip(circle, reals)]
            )
            real[q] = added([real[q], keep * sum_real])
            imaginary[q] = added([imaginary[q], keep * sum_imaginary])

    owner = [owners[0, q, 0] for q in range(scan_rows)]
    ranking = [
        sum([(owner[p] == owner[q]).astype(jnp.int32) for p in range(q)], jnp.int32(0))
        for q in range(scan_rows)
    ]
    slot_copies = []
    for dr in list(range(1, rows)) + [0]:
        target = row_at(dr)
        for c in range(CAP):
            chosen = [
                jnp.where((owner[q] == target) & (ranking[q] == c), 1.0, 0.0).astype(f32)
                for q in range(scan_rows)
            ]
            slot_real = added([chosen[q] * real[q] for q in range(scan_rows)])
            slot_imaginary = added([chosen[q] * imaginary[q] for q in range(scan_rows)])
            if dr == 0:
                out[0, 0, c, rows_of(row), :columns] = slot_real
                out[0, 0, c, rows_of(row), columns:] = slot_imaginary
            else:
                slots[dr, c, :, :columns] = slot_real
                slots[dr, c, :, columns:] = slot_imaginary
        if dr:
            copy = pltpu.make_async_remote_copy(
                src_ref=slots.at[dr], dst_ref=out.at[0, 0, :, rows_of(row), :],
                send_sem=slot_send.at[dr], recv_sem=slot_recv.at[row],
                device_id=device(dr, 0), device_id_type=pl.DeviceIdType.MESH,
            )
            copy.start()
            slot_copies.append(copy)

    for dr in range(1, rows):
        pltpu.make_async_remote_copy(
            src_ref=slots.at[dr], dst_ref=out.at[0, 0, :, rows_of(row_at(dr)), :],
            send_sem=slot_send.at[dr], recv_sem=slot_recv.at[row_at(dr)],
            device_id=device(dr, 0), device_id_type=pl.DeviceIdType.MESH,
        ).wait_recv()
    for copy in masks + sends + slot_copies:
        copy.wait_send()


def fused(patterns, jitter, subpixel, kernels, intersection, owners, wigner):
    _, pixel_share, length = patterns.shape
    height, width = wigner.shape[1:]
    subs = lax.axis_size("sub")
    groups = lax.axis_size("det") * subs
    rows = lax.axis_size("row")
    columns = length // groups
    scan_rows = owners.shape[1]
    part = height // rows
    chunks = 4
    fast = fast_tables(length, groups, scan_rows)
    fast_high = fast.astype(bf16)
    fast_low = (fast - fast_high.astype(np.float32)).astype(bf16)
    vmem = pl.BlockSpec(memory_space=pltpu.VMEM)
    smem = pl.BlockSpec(memory_space=pltpu.SMEM)
    hbm = pl.BlockSpec(memory_space=pl.ANY)
    sizes = (rows, groups, subs, scan_rows, height, columns, chunks)
    mask_rows = -(-scan_rows // 8) * 8
    dma = pltpu.SemaphoreType.DMA
    return pl.pallas_call(
        functools.partial(fused_kernel, sizes),
        out_shape=jax.ShapeDtypeStruct((1, 1, CAP, height, 2 * columns), f32),
        in_specs=[hbm, smem, smem, smem, smem, smem, vmem, vmem, hbm, hbm, hbm, vmem],
        out_specs=vmem,
        scratch_shapes=[
            pltpu.VMEM((pixel_share, length), f32),
            pltpu.VMEM((2, height, pixel_share), f32),
            pltpu.VMEM((groups, length, 2 * columns), bf16),
            pltpu.VMEM((groups, length, 2 * columns), bf16),
            pltpu.VMEM((groups, height, 2 * columns), f32),
            pltpu.VMEM((rows, groups, part, 2 * columns), f32),
            pltpu.VMEM((rows, mask_rows, columns), f32),
            pltpu.VMEM((rows, CAP, part, 2 * columns), f32),
            dma((3 + chunks,)),
            dma((rows, groups)),
            dma((rows, groups)),
            dma((rows,)),
            dma((rows,)),
            dma((rows,)),
            dma((rows,)),
        ],
        compiler_params=pltpu.CompilerParams(
            collective_id=0, has_side_effects=True, vmem_limit_bytes=32 * 1024 * 1024
        ),
    )(
        patterns, jitter, subpixel, kernels, intersection, owners, wigner,
        jnp.asarray(inner_table(width, 128 // width)),
        jnp.asarray(row_tables(height, width, groups)),
        jnp.asarray(fast_high), jnp.asarray(fast_low),
        jnp.asarray(shift_tables(length, groups)),
    )


def per_device(patterns, jitter, subpixel, kernels, intersection, owners, wigner):
    _, pixel_share, length = patterns.shape
    height, width = wigner.shape[1:]
    groups = lax.axis_size(("det", "sub"))
    rows = lax.axis_size("row")
    one_block = groups == rows and pixel_share % 1024 == 0
    tiles = height % (8 * rows) == 0 and (length // groups) % 128 == 0 and 128 % width == 0
    form = fused if one_block and tiles else general
    return form(patterns, jitter, subpixel, kernels, intersection, owners, wigner)


def solution(mesh):
    return jax.shard_map(
        per_device,
        mesh=mesh,
        in_specs=(
            P(("grp", "row"), ("det", "sub"), None),
            P(("grp", "row")),
            P(("grp", "row")),
            P(),
            P(("det", "sub"), None, "row"),
            P(("det", "sub"), None, None),
            P(),
        ),
        out_specs=P(("grp", "det", "sub"), "row", None, None, None),
        check_vma=False,
    )
```

profile of v0, /device:TPU:0, one launch (start us, length us, event | category | flops | bytes accessed | tf_op | source)
XLA Modules:
  0.0 32.3 jit_solution(5119348135898467042)
XLA Ops:
  1.3 0.7 %copy.14.intersection = s32[1,4,1]{2,1,0:T(4,128)S(1)} copy(s32[1,4,1]{1,2,0:T(1,128)} %param.16) | data formatting | bytes 32 | tf_op args[4]
  2.0 0.7 %copy.15.owners = s32[1,4,1]{2,1,0:T(4,128)S(1)} copy(s32[1,4,1]{1,2,0:T(1,128)} %param.17) | data formatting | bytes 32 | tf_op args[5]
  2.8 0.8 %copy.13.kernels = f32[16,4]{1,0:T(8,128)S(1)} copy(f32[16,4]{0,1:T(4,128)} %param.15) | data formatting | bytes 512 | tf_op args[3]
  3.5 0.0 copy-start
  3.5 1.6 %copy-done = f32[1,1024,512]{2,1,0:T(8,128)S(1)} copy-done((f32[1,1024,512]{2,1,0:T(8,128)S(1)}, f32[1,1024,512]{2,1,0:T(8,128)}, u32[]{:S(2)}) %copy-start) | copy-done | bytes 2097176
  5.1 0.0 copy-start.1
  5.1 1.6 %copy-done.1 = f32[4,2,64,1024]{3,2,1,0:T(8,128)S(1)} copy-done((f32[4,2,64,1024]{3,2,1,0:T(8,128)S(1)}, f32[4,2,64,1024]{3,2,1,0:T(8,128)}, u32[]{:S(2)}) %copy-start.1) | copy-done | bytes 2097176
  6.7 0.0 copy-start.2
  6.7 1.2 %copy-done.2 = bf16[4,512,256]{2,1,0:T(8,128)(2,1)S(1)} copy-done((bf16[4,512,256]{2,1,0:T(8,128)(2,1)S(1)}, bf16[4,512,256]{2,1,0:T(8,128)(2,1)}, u32[]{:S(2)}) %copy-start.2) | copy-done | bytes 1048600
  7.9 0.0 copy-start.3
  7.9 1.2 %copy-done.3 = bf16[4,512,256]{2,1,0:T(8,128)(2,1)S(1)} copy-done((bf16[4,512,256]{2,1,0:T(8,128)(2,1)S(1)}, bf16[4,512,256]{2,1,0:T(8,128)(2,1)}, u32[]{:S(2)}) %copy-start.3) | copy-done | bytes 1048600
  9.2 0.0 copy-start.4
  9.2 0.9 %copy-done.4 = f32[4,2,32,128]{3,2,1,0:T(8,128)S(1)} copy-done((f32[4,2,32,128]{3,2,1,0:T(8,128)S(1)}, f32[4,2,32,128]{3,2,1,0:T(8,128)}, u32[]{:S(2)}) %copy-start.4) | copy-done | bytes 131096
  10.1 0.0 copy-start.5
  10.1 0.8 %copy-done.5 = f32[2,64,64]{2,1,0:T(8,128)S(1)} copy-done((f32[2,64,64]{2,1,0:T(8,128)S(1)}, f32[2,64,64]{2,1,0:T(8,128)}, u32[]{:S(2)}) %copy-start.5) | copy-done | bytes 32792
  10.9 0.0 copy-start.6
  10.9 0.8 %copy-done.6 = f32[64,256]{1,0:T(8,128)S(1)} copy-done((f32[64,256]{1,0:T(8,128)S(1)}, f32[64,256]{1,0:T(8,128)}, u32[]{:S(2)}) %copy-start.6) | copy-done | bytes 65560
  11.8 19.9 %shard_map.118 = f32[1,1,2,64,256]{4,3,2,1,0:T(8,128)S(1)} custom-call(f32[1,1024,512]{2,1,0:T(8,128)S(1)} %copy-done, s32[1]{0:T(128)S(6)} %copy.17.jitter, s32[1]{0:T(128)S(6)} %copy.18.subpixel, f32[16,4]{1,0:T(8,128)S(1)} %copy.13.kernels, s32[1,4,1]{2,1,0:T(4,128)S(1)} %copy.14.intersection, s32[1,4,1]{2,1,0:T(4,128)S(1)} %copy.15.owners, ...), custom_call_target="tpu_custom_call" | custom-call | tf_op jit(solution)/shard_map/pallas_call | solution.py:361
  31.7 0.7 %copy.19 = f32[1,1,2,64,256]{4,3,2,1,0:T(8,128)} copy(f32[1,1,2,64,256]{4,3,2,1,0:T(8,128)S(1)} %shard_map.118) | data formatting | bytes 262144
Async XLA Ops:
  3.5 1.6 %copy-start = (f32[1,1024,512]{2,1,0:T(8,128)S(1)}, f32[1,1024,512]{2,1,0:T(8,128)}, u32[]{:S(2)}) copy-start(f32[1,1024,512]{2,1,0:T(8,128)} %patterns.1) | copy-start | bytes 6291460
  5.1 1.6 %copy-start.1 = (f32[4,2,64,1024]{3,2,1,0:T(8,128)S(1)}, f32[4,2,64,1024]{3,2,1,0:T(8,128)}, u32[]{:S(2)}) copy-start(f32[4,2,64,1024]{3,2,1,0:T(8,128)} %constant.11.clone.turns) | copy-start | bytes 6291460
  6.7 1.2 %copy-start.2 = (bf16[4,512,256]{2,1,0:T(8,128)(2,1)S(1)}, bf16[4,512,256]{2,1,0:T(8,128)(2,1)}, u32[]{:S(2)}) copy-start(bf16[4,512,256]{2,1,0:T(8,128)(2,1)} %constant.13.clone.fast_low) | copy-start | bytes 3145732
  7.9 1.2 %copy-start.3 = (bf16[4,512,256]{2,1,0:T(8,128)(2,1)S(1)}, bf16[4,512,256]{2,1,0:T(8,128)(2,1)}, u32[]{:S(2)}) copy-start(bf16[4,512,256]{2,1,0:T(8,128)(2,1)} %constant.12.clone.fast_high) | copy-start | bytes 3145732
  9.2 0.9 %copy-start.4 = (f32[4,2,32,128]{3,2,1,0:T(8,128)S(1)}, f32[4,2,32,128]{3,2,1,0:T(8,128)}, u32[]{:S(2)}) copy-start(f32[4,2,32,128]{3,2,1,0:T(8,128)} %constant.14.clone.phases) | copy-start | bytes 393220
  10.1 0.8 %copy-start.5 = (f32[2,64,64]{2,1,0:T(8,128)S(1)}, f32[2,64,64]{2,1,0:T(8,128)}, u32[]{:S(2)}) copy-start(f32[2,64,64]{2,1,0:T(8,128)} %wigner.1) | copy-start | bytes 98308
  10.9 0.8 %copy-start.6 = (f32[64,256]{1,0:T(8,128)S(1)}, f32[64,256]{1,0:T(8,128)}, u32[]{:S(2)}) copy-start(f32[64,256]{1,0:T(8,128)} %constant.10.clone.inner) | copy-start | bytes 196612
where the time goes:
time: 32.8 us; the launch traced here: 32.3 us
  Pallas kernels  19.9 us (61%)
  local copies, waits for them, and re-layouts  11.1 us (34%)
  between operations  1.31 us (4%)
    pallas_call x1, Pallas kernels, fused(): pl.pallas_call(functools.partial(fused_kernel, sizes), out_shape=jax.Shap...  19.9 us
    unnamed x18, local copies, waits for them, and re-layouts  11.1 us

commit v1 on v0

--- a/solution.py
+++ b/solution.py
@@ -141,8 +141,10 @@
 
 def fused_kernel(
     sizes, patterns, jitter, subpixel, kernels, intersection, owners, wigner, inner, turns,
-    fast_high, fast_low, phases, out, pixels, turn, table_high, table_low, outgoing, incoming,
-    visible, slots, load_sem, send_sem, recv_sem, mask_send, mask_recv, slot_send, slot_recv,
+    fast_high, fast_low, phases, out, kernels_here, intersection_here,
+    owners_here, wigner_here, inner_here, phases_here, pixels, turn, table_high, table_low, outgoing,
+    incoming, visible, slots, small_sem, load_sem, send_sem, recv_sem, mask_send, mask_recv,
+    slot_send, slot_recv,
 ):
     rows, groups, subs, scan_rows, height, columns, chunks = sizes
     row = lax.axis_index("row")
@@ -175,6 +177,17 @@
         )
         for k in range(chunks)
     ]
+    small = [
+        pltpu.make_async_copy(source, target, small_sem.at[k])
+        for k, (source, target) in enumerate(
+            [
+                (wigner, wigner_here), (inner, inner_here), (kernels, kernels_here),
+                (intersection, intersection_here), (owners, owners_here), (phases, phases_here),
+            ]
+        )
+    ]
+    for copy in small:
+        copy.start()
     loads[0].start()
     for piece in pieces:
         piece.start()
@@ -187,12 +200,14 @@
             barrier, inc=1, device_id=device(dr, dg), device_id_type=pl.DeviceIdType.MESH
         )
 
-    filter_real, filter_imaginary = wiener_parts(wigner[0], wigner[1])
+    small[0].wait()
+    small[1].wait()
+    filter_real, filter_imaginary = wiener_parts(wigner_here[0], wigner_here[1])
     both = jnp.dot(
-        jnp.concatenate([filter_real, filter_imaginary]), inner[...],
+        jnp.concatenate([filter_real, filter_imaginary]), inner_here[...],
         precision=highest, preferred_element_type=f32,
     )
-    lanes = inner.shape[1] // 2
+    lanes = inner_here.shape[1] // 2
     inner_real = both[:height, :lanes] + both[height:, lanes:]
     inner_imaginary = both[height:, :lanes] - both[:height, lanes:]
     loads[0].wait()
@@ -218,18 +233,20 @@
         folded = folded + (times(high, piece_high) + times(high, piece_low) + times(low, piece_high))
     folded_high, folded_low = split(folded)
 
+    for copy in small[2:]:
+        copy.wait()
     shifts = lax.broadcasted_iota(jnp.int32, (SHIFTS, columns), 0) - SHIFTS // 2
-    taps = kernels.shape[1]
+    taps = kernels.shape[0]
     weight = jnp.zeros((SHIFTS, columns), f32)
     for t in range(taps):
         weight = weight + jnp.where(
-            shifts == jitter[0] + (t - taps // 2), kernels[subpixel[0], t], 0.0
+            shifts == jitter[0] + (t - taps // 2), kernels_here[t, subpixel[0]], 0.0
         )
 
     frequency = lax.broadcasted_iota(jnp.int32, visible.shape[1:], 0)
     tile = jnp.zeros(visible.shape[1:], f32)
     for q in range(scan_rows):
-        tile = jnp.where(frequency == q, intersection[0, q, 0].astype(f32), tile)
+        tile = jnp.where(frequency == q, intersection_here[0, q].astype(f32), tile)
     visible[row] = tile
 
     pl.semaphore_wait(barrier, len(peers))
@@ -251,8 +268,8 @@
         product = times(folded_high, high) + times(folded_high, table_low[other]) + times(folded_low, high)
         real = product[:height, :columns] + product[height:, columns:]
         imaginary = product[height:, :columns] - product[:height, columns:]
-        phase_real = jnp.sum(weight * phases[other, 0], axis=0, keepdims=True)
-        phase_imaginary = jnp.sum(weight * phases[other, 1], axis=0, keepdims=True)
+        phase_real = jnp.sum(weight * phases_here[other, 0], axis=0, keepdims=True)
+        phase_imaginary = jnp.sum(weight * phases_here[other, 1], axis=0, keepdims=True)
         outgoing[dg, :, :columns] = real * phase_real - imaginary * phase_imaginary
         outgoing[dg, :, columns:] = real * phase_imaginary + imaginary * phase_real
         for dr in range(rows):
@@ -299,7 +316,7 @@
             real[q] = added([real[q], keep * sum_real])
             imaginary[q] = added([imaginary[q], keep * sum_imaginary])
 
-    owner = [owners[0, q, 0] for q in range(scan_rows)]
+    owner = [owners_here[0, q] for q in range(scan_rows)]
     ranking = [
         sum([(owner[p] == owner[q]).astype(jnp.int32) for p in range(q)], jnp.int32(0))
         for q in range(scan_rows)
@@ -361,9 +378,15 @@
     return pl.pallas_call(
         functools.partial(fused_kernel, sizes),
         out_shape=jax.ShapeDtypeStruct((1, 1, CAP, height, 2 * columns), f32),
-        in_specs=[hbm, smem, smem, smem, smem, smem, vmem, vmem, hbm, hbm, hbm, vmem],
+        in_specs=[hbm, smem, smem] + [hbm] * 9,
         out_specs=vmem,
         scratch_shapes=[
+            pltpu.SMEM(kernels.shape[::-1], f32),
+            pltpu.SMEM((1, scan_rows), jnp.int32),
+            pltpu.SMEM((1, scan_rows), jnp.int32),
+            pltpu.VMEM(wigner.shape, f32),
+            pltpu.VMEM((width, 256), f32),
+            pltpu.VMEM((groups, 2, SHIFTS, columns), f32),
             pltpu.VMEM((pixel_share, length), f32),
             pltpu.VMEM((2, height, pixel_share), f32),
             pltpu.VMEM((groups, length, 2 * columns), bf16),
@@ -372,6 +395,7 @@
             pltpu.VMEM((rows, groups, part, 2 * columns), f32),
             pltpu.VMEM((rows, mask_rows, columns), f32),
             pltpu.VMEM((rows, CAP, part, 2 * columns), f32),
+            dma((6,)),
             dma((3 + chunks,)),
             dma((rows, groups)),
             dma((rows, groups)),
@@ -381,10 +405,11 @@
             dma((rows,)),
         ],
         compiler_params=pltpu.CompilerParams(
-            collective_id=0, has_side_effects=True, vmem_limit_bytes=32 * 1024 * 1024
+            collective_id=0, has_side_effects=True, vmem_limit_bytes=60 * 1024 * 1024
         ),
     )(
-        patterns, jitter, subpixel, kernels, intersection, owners, wigner,
+        patterns, jitter, subpixel, kernels.T, intersection.reshape(1, scan_rows),
+        owners.reshape(1, scan_rows), wigner,
         jnp.asarray(inner_table(width, 128 // width)),
         jnp.asarray(row_tables(height, width, groups)),
         jnp.asarray(fast_high), jnp.asarray(fast_low),

time: 32.8 us -> 22.6 us (0.69)
  local copies, waits for them, and re-layouts: 11.1 us -> 1.57 us
    unnamed x18 -> x1, local copies, waits for them, and re-layouts: 11.1 us -> 1.57 us
    pallas_call x1, Pallas kernels: 19.9 us -> 19.6 us  [fused(): pl.pallas_call(functools.partial(fused_kernel, sizes), out_shape=jax.Shap...]
where the time goes in v1:
time: 22.6 us; the launch traced here: 22.5 us
  Pallas kernels  19.6 us (87%)
  local copies, waits for them, and re-layouts  1.57 us (7%)
  between operations  1.3 us (6%)
    pallas_call x1, Pallas kernels, fused(): pl.pallas_call(functools.partial(fused_kernel, sizes), out_shape=jax.Shap...  19.6 us
    unnamed x1, local copies, waits for them, and re-layouts  1.57 us

profile of v1, /device:TPU:0, one launch (start us, length us, event | category | flops | bytes accessed | tf_op | source)
XLA Modules:
  0.0 22.5 jit_solution(8775752830936633525)
XLA Ops:
  1.3 19.6 %shard_map.118 = f32[1,1,2,64,256]{4,3,2,1,0:T(8,128)} custom-call(f32[1,1024,512]{2,1,0:T(8,128)} %patterns.1, s32[1]{0:T(128)S(6)} %copy.14.jitter, s32[1]{0:T(128)S(6)} %copy.15.subpixel, f32[4,16]{1,0:T(4,128)} %bitcast.3, s32[1,4]{1,0:T(1,128)} %bitcast.4, s32[1,4]{1,0:T(1,128)} %bitcast.5, f32[2,64,64]{2,1,0:T(8,128)} %wigner.1, ...), custom_call_target="tpu_custom_call" | custom-call | tf_op jit(solution)/shard_map/pallas_call | solution.py:378
  20.9 1.6 %copy.16 = f32[1,1,2,64,256]{4,3,2,1,0:T(8,128)} copy(f32[1,1,2,64,256]{4,3,2,1,0:T(8,128)} %shard_map.118) | data formatting | bytes 262144

commit v2 on v1

--- a/solution.py
+++ b/solution.py
@@ -143,27 +143,49 @@
     sizes, patterns, jitter, subpixel, kernels, intersection, owners, wigner, inner, turns,
     fast_high, fast_low, phases, out, kernels_here, intersection_here,
     owners_here, wigner_here, inner_here, phases_here, pixels, turn, table_high, table_low, outgoing,
-    incoming, visible, slots, small_sem, load_sem, send_sem, recv_sem, mask_send, mask_recv,
+    incoming, visible, slots, arrivals, small_sem, load_sem, send_sem, recv_sem, mask_send, mask_recv,
     slot_send, slot_recv,
 ):
-    rows, groups, subs, scan_rows, height, columns, chunks = sizes
+    rows, dets, subs, scan_rows, height, columns, chunks, parts = sizes
+    groups = dets * subs
     row = lax.axis_index("row")
-    group = lax.axis_index("det") * subs + lax.axis_index("sub")
-    part = height // rows
-    peers = [(dr, dg) for dg in range(groups) for dr in range(rows) if (dr, dg) != (0, 0)]
+    det = lax.axis_index("det")
+    sub = lax.axis_index("sub")
+    group = det * subs + sub
+    pair = row // 2
+    side = row - 2 * pair
+    share = height // 2
+    part = share // parts
+
+    def wrapped(index, size):
+        return jnp.where(index >= size, index - size, index)
+
+    row_of = [row, 2 * pair + 1 - side, 2 * (1 - pair) + side, 2 * (1 - pair) + 1 - side]
+    side_of = [side, 1 - side]
+    det_of = [det] + [wrapped(det + k, dets) for k in range(1, dets)]
+    sub_of = [sub] + [wrapped(sub + k, subs) for k in range(1, subs)]
+    group_of = [d * subs + u for d in det_of for u in sub_of]
+    group_order = list(range(groups))[::-1]
+    near = [(m, dg) for dg in group_order for m in (1, 0) if (m, dg) != (0, 0)]
+    peers = [(3, 0), (2, 0)] + near
 
     def row_at(offset):
-        return lax.rem(row + offset, rows)
+        return row_of[offset]
 
     def group_at(offset):
-        return lax.rem(group + offset, groups)
+        return group_of[offset]
 
     def device(dr, dg):
-        other = group_at(dg)
-        return {"row": row_at(dr), "det": other // subs, "sub": lax.rem(other, subs)}
-
-    def rows_of(index):
-        return pl.ds(pl.multiple_of(index * part, part), part)
+        return {"row": row_of[dr], "det": det_of[dg // subs], "sub": sub_of[dg % subs]}
+
+    def rows_of(which, c):
+        return pl.ds(pl.multiple_of(which * share + c * part, part), part)
+
+    barrier = pltpu.get_barrier_semaphore()
+    for dr, dg in peers:
+        pl.semaphore_signal(
+            barrier, inc=1, device_id=device(dr, dg), device_id_type=pl.DeviceIdType.MESH
+        )
 
     chunk = pixels.shape[0] // chunks
     loads = [
@@ -193,12 +215,6 @@
         piece.start()
     loads[1].start()
     loads[2].start()
-
-    barrier = pltpu.get_barrier_semaphore()
-    for dr, dg in peers:
-        pl.semaphore_signal(
-            barrier, inc=1, device_id=device(dr, dg), device_id_type=pl.DeviceIdType.MESH
-        )
 
     small[0].wait()
     small[1].wait()
@@ -262,7 +278,21 @@
     loads[1].wait()
     loads[2].wait()
     sends = []
-    for dg in list(range(1, groups)) + [0]:
+
+    def send(c, dg):
+        for m in (1, 0):
+            if (m, dg) == (0, 0):
+                incoming[c, side, group] = outgoing[0, rows_of(side, c), :]
+                continue
+            copy = pltpu.make_async_remote_copy(
+                src_ref=outgoing.at[dg, rows_of(side_of[m], c), :], dst_ref=incoming.at[c, side, group],
+                send_sem=send_sem.at[c, m, dg], recv_sem=recv_sem.at[c, side, group],
+                device_id=device(m, dg), device_id_type=pl.DeviceIdType.MESH,
+            )
+            copy.start()
+            sends.append(copy)
+
+    for dg in group_order:
         other = group_at(dg)
         high = table_high[other]
         product = times(folded_high, high) + times(folded_high, table_low[other]) + times(folded_low, high)
@@ -272,86 +302,89 @@
         phase_imaginary = jnp.sum(weight * phases_here[other, 1], axis=0, keepdims=True)
         outgoing[dg, :, :columns] = real * phase_real - imaginary * phase_imaginary
         outgoing[dg, :, columns:] = real * phase_imaginary + imaginary * phase_real
-        for dr in range(rows):
-            if (dr, dg) == (0, 0):
-                incoming[row, group] = outgoing[0, rows_of(row), :]
-                continue
-            copy = pltpu.make_async_remote_copy(
-                src_ref=outgoing.at[dg, rows_of(row_at(dr)), :], dst_ref=incoming.at[row, group],
-                send_sem=send_sem.at[dr, dg], recv_sem=recv_sem.at[row, group],
-                device_id=device(dr, dg), device_id_type=pl.DeviceIdType.MESH,
-            )
-            copy.start()
-            sends.append(copy)
-
-    for dr in range(1, rows):
-        pltpu.make_async_remote_copy(
-            src_ref=visible.at[row_at(dr)], dst_ref=visible.at[row_at(dr)], send_sem=mask_send.at[dr],
-            recv_sem=mask_recv.at[row_at(dr)], device_id=device(dr, 0), device_id_type=pl.DeviceIdType.MESH,
-        ).wait_recv()
-    for dr, dg in peers:
-        pltpu.make_async_remote_copy(
-            src_ref=outgoing.at[dg, rows_of(row), :], dst_ref=incoming.at[row_at(dr), group_at(dg)],
-            send_sem=send_sem.at[dr, dg], recv_sem=recv_sem.at[row_at(dr), group_at(dg)],
-            device_id=device(dr, dg), device_id_type=pl.DeviceIdType.MESH,
-        ).wait_recv()
-
-    real = [None] * scan_rows
-    imaginary = [None] * scan_rows
-    for b in range(groups):
-        values = [incoming[y, b] for y in range(rows)]
-        reals = [v[:, :columns] for v in values]
-        imaginaries = [v[:, columns:] for v in values]
-        for q in range(scan_rows):
-            circle = [unit_circle(np.array(q * y), rows) for y in range(rows)]
-            keep = visible[b, q : q + 1, :]
-            sum_real = added(
-                [scaled(c, v) for (c, _), v in zip(circle, reals)]
-                + [scaled(s, v) for (_, s), v in zip(circle, imaginaries)]
-            )
-            sum_imaginary = added(
-                [scaled(c, v) for (c, _), v in zip(circle, imaginaries)]
-                + [scaled(-s, v) for (_, s), v in zip(circle, reals)]
-            )
-            real[q] = added([real[q], keep * sum_real])
-            imaginary[q] = added([imaginary[q], keep * sum_imaginary])
+        send(0, dg)
+    for c in range(1, parts):
+        for dg in group_order:
+            send(c, dg)
 
     owner = [owners_here[0, q] for q in range(scan_rows)]
     ranking = [
         sum([(owner[p] == owner[q]).astype(jnp.int32) for p in range(q)], jnp.int32(0))
         for q in range(scan_rows)
     ]
+    sign = (1 - 2 * pair).astype(f32)
+    chosen = {
+        (m, k, q): jnp.where(
+            (owner[q] == row_of[m]) & (ranking[q] == k), sign if q % 2 else jnp.float32(1.0), 0.0
+        )
+        for m in range(rows) for k in range(CAP) for q in range(scan_rows)
+    }
+
+    for m in range(1, rows):
+        pltpu.make_async_remote_copy(
+            src_ref=visible.at[row_at(m)], dst_ref=visible.at[row_at(m)], send_sem=mask_send.at[m],
+            recv_sem=mask_recv.at[row_at(m)], device_id=device(m, 0), device_id_type=pl.DeviceIdType.MESH,
+        ).wait_recv()
+
     slot_copies = []
-    for dr in list(range(1, rows)) + [0]:
-        target = row_at(dr)
-        for c in range(CAP):
-            chosen = [
-                jnp.where((owner[q] == target) & (ranking[q] == c), 1.0, 0.0).astype(f32)
-                for q in range(scan_rows)
-            ]
-            slot_real = added([chosen[q] * real[q] for q in range(scan_rows)])
-            slot_imaginary = added([chosen[q] * imaginary[q] for q in range(scan_rows)])
-            if dr == 0:
-                out[0, 0, c, rows_of(row), :columns] = slot_real
-                out[0, 0, c, rows_of(row), columns:] = slot_imaginary
-            else:
-                slots[dr, c, :, :columns] = slot_real
-                slots[dr, c, :, columns:] = slot_imaginary
-        if dr:
-            copy = pltpu.make_async_remote_copy(
-                src_ref=slots.at[dr], dst_ref=out.at[0, 0, :, rows_of(row), :],
-                send_sem=slot_send.at[dr], recv_sem=slot_recv.at[row],
-                device_id=device(dr, 0), device_id_type=pl.DeviceIdType.MESH,
-            )
-            copy.start()
-            slot_copies.append(copy)
-
-    for dr in range(1, rows):
-        pltpu.make_async_remote_copy(
-            src_ref=slots.at[dr], dst_ref=out.at[0, 0, :, rows_of(row_at(dr)), :],
-            send_sem=slot_send.at[dr], recv_sem=slot_recv.at[row_at(dr)],
-            device_id=device(dr, 0), device_id_type=pl.DeviceIdType.MESH,
-        ).wait_recv()
+    for c in range(parts):
+        for m, dg in near:
+            pltpu.make_async_remote_copy(
+                src_ref=outgoing.at[dg, rows_of(side, c), :],
+                dst_ref=incoming.at[c, side_of[m], group_at(dg)],
+                send_sem=send_sem.at[c, m, dg], recv_sem=recv_sem.at[c, side_of[m], group_at(dg)],
+                device_id=device(m, dg), device_id_type=pl.DeviceIdType.MESH,
+            ).wait_recv()
+
+        real = [None] * scan_rows
+        imaginary = [None] * scan_rows
+        for b in range(groups):
+            values = [incoming[c, y, b] for y in range(2)]
+            reals = [v[:, :columns] for v in values]
+            imaginaries = [v[:, columns:] for v in values]
+            for q in range(scan_rows):
+                circle = [unit_circle(np.array(q * y), rows) for y in range(2)]
+                keep = visible[b, q : q + 1, :]
+                sum_real = added(
+                    [scaled(c_, v) for (c_, _), v in zip(circle, reals)]
+                    + [scaled(s_, v) for (_, s_), v in zip(circle, imaginaries)]
+                )
+                sum_imaginary = added(
+                    [scaled(c_, v) for (c_, _), v in zip(circle, imaginaries)]
+                    + [scaled(-s_, v) for (_, s_), v in zip(circle, reals)]
+                )
+                real[q] = added([real[q], keep * sum_real])
+                imaginary[q] = added([imaginary[q], keep * sum_imaginary])
+
+        for m in (3, 2, 1, 0):
+            for k in range(CAP):
+                slot_real = added([chosen[m, k, q] * real[q] for q in range(scan_rows)])
+                slot_imaginary = added([chosen[m, k, q] * imaginary[q] for q in range(scan_rows)])
+                if m == 0:
+                    arrivals[c, row, k, :, :columns] = slot_real
+                    arrivals[c, row, k, :, columns:] = slot_imaginary
+                else:
+                    slots[c, m, k, :, :columns] = slot_real
+                    slots[c, m, k, :, columns:] = slot_imaginary
+            if m:
+                copy = pltpu.make_async_remote_copy(
+                    src_ref=slots.at[c, m], dst_ref=arrivals.at[c, row],
+                    send_sem=slot_send.at[c, m], recv_sem=slot_recv.at[c, row],
+                    device_id=device(m, 0), device_id_type=pl.DeviceIdType.MESH,
+                )
+                copy.start()
+                slot_copies.append(copy)
+
+    for c in range(parts):
+        for m in range(1, rows):
+            pltpu.make_async_remote_copy(
+                src_ref=slots.at[c, m], dst_ref=arrivals.at[c, row_at(m)],
+                send_sem=slot_send.at[c, m], recv_sem=slot_recv.at[c, row_at(m)],
+                device_id=device(m, 0), device_id_type=pl.DeviceIdType.MESH,
+            ).wait_recv()
+        for y in range(2):
+            first = y * share + c * part
+            out[0, 0, :, first : first + part, :] = arrivals[c, y] + arrivals[c, y + 2]
     for copy in masks + sends + slot_copies:
         copy.wait_send()
 
@@ -360,19 +393,21 @@
     _, pixel_share, length = patterns.shape
     height, width = wigner.shape[1:]
     subs = lax.axis_size("sub")
-    groups = lax.axis_size("det") * subs
+    dets = lax.axis_size("det")
+    groups = dets * subs
     rows = lax.axis_size("row")
     columns = length // groups
     scan_rows = owners.shape[1]
-    part = height // rows
     chunks = 4
+    parts = 2
+    part = height // 2 // parts
     fast = fast_tables(length, groups, scan_rows)
     fast_high = fast.astype(bf16)
     fast_low = (fast - fast_high.astype(np.float32)).astype(bf16)
     vmem = pl.BlockSpec(memory_space=pltpu.VMEM)
     smem = pl.BlockSpec(memory_space=pltpu.SMEM)
     hbm = pl.BlockSpec(memory_space=pl.ANY)
-    sizes = (rows, groups, subs, scan_rows, height, columns, chunks)
+    sizes = (rows, dets, subs, scan_rows, height, columns, chunks, parts)
     mask_rows = -(-scan_rows // 8) * 8
     dma = pltpu.SemaphoreType.DMA
     return pl.pallas_call(
@@ -392,17 +427,18 @@
             pltpu.VMEM((groups, length, 2 * columns), bf16),
             pltpu.VMEM((groups, length, 2 * columns), bf16),
             pltpu.VMEM((groups, height, 2 * columns), f32),
-            pltpu.VMEM((rows, groups, part, 2 * columns), f32),
+            pltpu.VMEM((parts, 2, groups, part, 2 * columns), f32),
             pltpu.VMEM((rows, mask_rows, columns), f32),
-            pltpu.VMEM((rows, CAP, part, 2 * columns), f32),
+            pltpu.VMEM((parts, rows, CAP, part, 2 * columns), f32),
+            pltpu.VMEM((parts, rows, CAP, part, 2 * columns), f32),
             dma((6,)),
             dma((3 + chunks,)),
-            dma((rows, groups)),
-            dma((rows, groups)),
+            dma((parts, 2, groups)),
+            dma((parts, 2, groups)),
             dma((rows,)),
             dma((rows,)),
-            dma((rows,)),
-            dma((rows,)),
+            dma((parts, rows)),
+            dma((parts, rows)),
         ],
         compiler_params=pltpu.CompilerParams(
             collective_id=0, has_side_effects=True, vmem_limit_bytes=60 * 1024 * 1024
@@ -422,8 +458,8 @@
     height, width = wigner.shape[1:]
     groups = lax.axis_size(("det", "sub"))
     rows = lax.axis_size("row")
-    one_block = groups == rows and pixel_share % 1024 == 0
-    tiles = height % (8 * rows) == 0 and (length // groups) % 128 == 0 and 128 % width == 0
+    one_block = groups == rows == owners.shape[1] == 4 and pixel_share % 1024 == 0
+    tiles = height % 64 == 0 and (length // groups) % 128 == 0 and 128 % width == 0
     form = fused if one_block and tiles else general
     return form(patterns, jitter, subpixel, kernels, intersection, owners, wigner)
 

time: 22.6 us -> 22.2 us (0.982)
  Pallas kernels: 19.6 us -> 19.1 us
    pallas_call x1, Pallas kernels: 19.6 us -> 19.1 us  [fused(): pl.pallas_call(functools.partial(fused_kernel, sizes), out_shape=jax.Shap...]
where the time goes in v2:
time: 22.2 us; the launch traced here: 22 us
  Pallas kernels  19.1 us (86%)
  local copies, waits for them, and re-layouts  1.57 us (7%)
  between operations  1.3 us (6%)
    pallas_call x1, Pallas kernels, fused(): pl.pallas_call(functools.partial(fused_kernel, sizes), out_shape=jax.Shap...  19.1 us
    unnamed x1, local copies, waits for them, and re-layouts  1.57 us

profile of v2, /device:TPU:0, one launch (start us, length us, event | category | flops | bytes accessed | tf_op | source)
XLA Modules:
  0.0 22.0 jit_solution(14982571854610121308)
XLA Ops:
  1.3 19.1 %shard_map.118 = f32[1,1,2,64,256]{4,3,2,1,0:T(8,128)} custom-call(f32[1,1024,512]{2,1,0:T(8,128)} %patterns.1, s32[1]{0:T(128)S(6)} %copy.14.jitter, s32[1]{0:T(128)S(6)} %copy.15.subpixel, f32[4,16]{1,0:T(4,128)} %bitcast.3, s32[1,4]{1,0:T(1,128)} %bitcast.4, s32[1,4]{1,0:T(1,128)} %bitcast.5, f32[2,64,64]{2,1,0:T(8,128)} %wigner.1, ...), custom_call_target="tpu_custom_call" | custom-call | tf_op jit(solution)/shard_map/pallas_call | solution.py:413
  20.4 1.6 %copy.16 = f32[1,1,2,64,256]{4,3,2,1,0:T(8,128)} copy(f32[1,1,2,64,256]{4,3,2,1,0:T(8,128)} %shard_map.118) | data formatting | bytes 262144

commit v3 on v2

--- a/solution.py
+++ b/solution.py
@@ -384,7 +384,8 @@
             ).wait_recv()
         for y in range(2):
             first = y * share + c * part
-            out[0, 0, :, first : first + part, :] = arrivals[c, y] + arrivals[c, y + 2]
+            for h in range(2):
+                out[h, :, first : first + part, :] = arrivals[c, y + 2 * h]
     for copy in masks + sends + slot_copies:
         copy.wait_send()
 
@@ -410,9 +411,9 @@
     sizes = (rows, dets, subs, scan_rows, height, columns, chunks, parts)
     mask_rows = -(-scan_rows // 8) * 8
     dma = pltpu.SemaphoreType.DMA
-    return pl.pallas_call(
+    halves = pl.pallas_call(
         functools.partial(fused_kernel, sizes),
-        out_shape=jax.ShapeDtypeStruct((1, 1, CAP, height, 2 * columns), f32),
+        out_shape=jax.ShapeDtypeStruct((2, CAP, height, 2 * columns), f32),
         in_specs=[hbm, smem, smem] + [hbm] * 9,
         out_specs=vmem,
         scratch_shapes=[
@@ -451,6 +452,7 @@
         jnp.asarray(fast_high), jnp.asarray(fast_low),
         jnp.asarray(shift_tables(length, groups)),
     )
+    return (halves[0] + halves[1])[None, None]
 
 
 def per_device(patterns, jitter, subpixel, kernels, intersection, owners, wigner):

time: 22.2 us -> 22.3 us (level)
  other arithmetic: 0 us -> 1.64 us
  local copies, waits for them, and re-layouts: 1.57 us -> 0 us
    add x0 -> x1, other arithmetic: none -> 1.64 us  [fused(): return (halves[0] + halves[1])[None, None]]
    unnamed x1 -> x0, local copies, waits for them, and re-layouts: 1.57 us -> none
where the time goes in v3:
time: 22.3 us; the launch traced here: 22.1 us
  Pallas kernels  19.2 us (86%)
  other arithmetic  1.64 us (7%)
  between operations  1.3 us (6%)
    pallas_call x1, Pallas kernels, fused(): pl.pallas_call(functools.partial(fused_kernel, sizes), out_shape=jax.Shap...  19.2 us
    add x1, other arithmetic, fused(): return (halves[0] + halves[1])[None, None]  1.64 us

profile of v3, /device:TPU:0, one launch (start us, length us, event | category | flops | bytes accessed | tf_op | source)
XLA Modules:
  0.0 22.1 jit_solution(14701285339898156533)
XLA Ops:
  1.3 19.2 %shard_map.118 = f32[2,2,64,256]{3,2,1,0:T(8,128)} custom-call(f32[1,1024,512]{2,1,0:T(8,128)} %patterns.1, s32[1]{0:T(128)S(6)} %copy.13.jitter, s32[1]{0:T(128)S(6)} %copy.14.subpixel, f32[4,16]{1,0:T(4,128)} %bitcast.5, s32[1,4]{1,0:T(1,128)} %bitcast.6, s32[1,4]{1,0:T(1,128)} %bitcast.7, f32[2,64,64]{2,1,0:T(8,128)} %wigner.1, ...), custom_call_target="tpu_custom_call" | custom-call | tf_op jit(solution)/shard_map/pallas_call | solution.py:414
  20.5 1.6 %add_bitcast_fusion = f32[1,1,2,64,256]{4,3,2,1,0:T(8,128)} fusion(f32[2,2,64,256]{3,2,1,0:T(8,128)} %shard_map.118), kind=kLoop, calls=%fused_computation | loop fusion | flops 32768 | bytes 393216 | tf_op jit(solution)/shard_map/add | solution.py:455
